TPU v7x, 32 devices: a whole 2x2x4 slice. The times are simulated.
32 devices in a mesh: grp: 4 (over x, core), mem: 8 (over z, y).
Axes of the slice: x: 2, y: 2, z: 4, core: 2. Of those that a mesh axis runs over, the one named last changes fastest.
Arguments:
- vertex_table: float32 [32768, 128], P(('grp', 'mem')), may hold values from -1.8 to 1.8
- context_table: float32 [32768, 128], P(('grp', 'mem')), may hold values from -1.8 to 1.8
- edge_source: int32 [4, 4, 64, 512], P(None, 'grp', 'mem'), may hold values from 0 to 127
- edge_target: int32 [4, 4, 64, 512], P(None, 'grp', 'mem'), may hold values from 0 to 1534, as said below
- edge_weight: int32 [4, 4, 64, 512], P(None, 'grp', 'mem'), may hold values from 0 to 4, as said below
- negative_rows: int32 [4, 4, 64, 5, 512], P(None, 'grp', 'mem'), may hold values from 0 to 1535
Outputs:
- vertex_final: float32 [32768, 128], P(('grp', 'mem'))
- context_final: float32 [32768, 128], P(('grp', 'mem'))
Inputs may be any that keep to these rules, and one draw needn't show every extreme that they name: For the slot's vertex row r = b * 128 + edge_source within its device (tile b of the device), edge_target - 256 - r lies in -256 to 255. `edge_weight`: in each tile the slots of nonzero weight come first; in every stratum each device has a tile whose 512 slots all have nonzero weight.
All inputs are finite; a program needn't handle non-finite values.
Results may differ from a plain program's by a relative error of at most 0.00014.
Values sent between devices are 32-bit elements; how exact they have to be, the bound alone decides.
A program may use at most 128 MiB of HBM per device.

v0:
```python
import functools

import jax
import jax.numpy as jnp
from jax import lax
from jax.experimental import pallas as pl
from jax.experimental.pallas import tpu as pltpu
from jax.sharding import PartitionSpec as P

LR = 0.05
STRIP = 256
LANE = 256
BF = jnp.bfloat16
F32 = jnp.float32
NT = (((1,), (1,)), ((), ()))
NN = (((1,), (0,)), ((), ()))


def dot(a, b, dims=NN):
    return lax.dot_general(a, b, dims, preferred_element_type=F32)


def split(x):
    hi = x.astype(BF)
    return hi, (x - hi.astype(F32)).astype(BF)


def row_bf(x):
    return x.astype(F32).astype(BF)


def count_tile(b, src, tgt, w, neg, wneg, wpos, rowblk):
    slots = src.shape[1]
    chunks = wneg.shape[0]
    one = jnp.ones((), BF)
    zero = jnp.zeros((), BF)
    iota_r = row_bf(lax.broadcasted_iota(jnp.int32, (rowblk, slots), 0))
    iota_c = row_bf(lax.broadcasted_iota(jnp.int32, (LANE, slots), 0))
    s1 = jnp.where(iota_r == row_bf(src), row_bf(w), zero)

    def hot(x):
        return jnp.where(iota_c == row_bf(x & (LANE - 1)), one, zero)

    def tall(x, first, count):
        hi = (x >> 8) - first
        return jnp.concatenate(
            [s1 * row_bf(jnp.where(hi == h, 1.0, 0.0)) for h in range(count)], axis=0
        )

    at = jnp.concatenate([tall(neg[n : n + 1], 0, chunks) for n in range(neg.shape[0])], axis=1)
    bt = jnp.concatenate([hot(neg[n : n + 1]) for n in range(neg.shape[0])], axis=1)
    cn = dot(at, bt, NT)
    first = b // 2
    cp = dot(tall(tgt, first, 3), hot(tgt), NT)
    rows = pl.ds(pl.multiple_of(b * rowblk, rowblk), rowblk)
    for h in range(chunks):
        wneg[h, rows, :] = cn[h * rowblk : (h + 1) * rowblk]
    for h in range(3):
        wpos[first + h, rows, :] = cp[h * rowblk : (h + 1) * rowblk]


def flip(g, value):
    bit = 1
    while bit <= value:
        if value & bit:
            g = g + bit - 2 * bit * ((g // bit) % 2)
        bit *= 2
    return g


def gray(t):
    return t ^ (t >> 1)


def remote(src, dst, send, recv, **where):
    return pltpu.make_async_remote_copy(
        src_ref=src, dst_ref=dst, send_sem=send, recv_sem=recv,
        device_id=where, device_id_type=pl.DeviceIdType.MESH,
    )


def kernel(
    v_in, c_in, e_src, e_tgt, e_w, e_neg, vout, cout,
    wneg, wpos, r_src, r_tgt, r_w, r_neg, vnew, vrecv, gs, gr, gm, gv, cext, chalo, vcat, vtcat,
    edge_send, edge_recv, halo_send, halo_recv, rim_send, rim_recv, v_send, v_recv,
):
    strata, blocks, slots = e_src.shape
    rows, width = v_in.shape
    rowblk = rows // blocks
    chunks = wneg.shape[1]
    zone = 2 * STRIP
    g = lax.axis_index("grp")
    m = lax.axis_index("mem")
    members = lax.axis_size("mem")
    groups = lax.axis_size("grp")
    has_down = m > 0
    has_up = m < members - 1

    barrier = pltpu.get_barrier_semaphore()
    for k in range(1, groups):
        pl.semaphore_signal(barrier, inc=1, device_id={"grp": flip(g, k)}, device_id_type=pl.DeviceIdType.MESH)

    @pl.when(has_down)
    def _():
        pl.semaphore_signal(barrier, inc=1, device_id={"mem": m - 1}, device_id_type=pl.DeviceIdType.MESH)

    @pl.when(has_up)
    def _():
        pl.semaphore_signal(barrier, inc=1, device_id={"mem": m + 1}, device_id_type=pl.DeviceIdType.MESH)

    pl.semaphore_wait(barrier, groups - 1 + jnp.where(has_down, 1, 0) + jnp.where(has_up, 1, 0))

    def halo(side):
        if side == 0:
            return remote(c_in.at[0:STRIP], chalo.at[1], halo_send.at[0], halo_recv.at[1], mem=m - 1)
        return remote(c_in.at[rows - STRIP : rows], chalo.at[0], halo_send.at[1], halo_recv.at[0], mem=m + 1)

    def rim(t, side):
        last = t == strata - 1
        if side == 0:
            span = slice(0, STRIP if last else zone)
            return remote(gs.at[t, 0, span], gr.at[t, 1, span], rim_send.at[t, 0], rim_recv.at[t, 1], mem=m - 1)
        span = slice(STRIP if last else 0, zone)
        return remote(gs.at[t, 1, span], gr.at[t, 0, span], rim_send.at[t, 1], rim_recv.at[t, 0], mem=m + 1)

    def hop(t, part):
        step = gray(t) ^ gray((t + 1) % strata)
        span = slice(part * rows // 2, (part + 1) * rows // 2)
        return remote(
            vnew.at[t, span], vrecv.at[t, span], v_send.at[t, part], v_recv.at[t, part], grp=flip(g, step)
        )

    def edge(t, k):
        a = (e_src, e_tgt, e_w, e_neg)[k]
        z = (r_src, r_tgt, r_w, r_neg)[k]
        i = (t - 1) * 4 + k
        return remote(a.at[t], z.at[t - 1], edge_send.at[i], edge_recv.at[i], grp=flip(g, gray(t)))

    def both(action):
        @pl.when(has_down)
        def _():
            action(0)

        @pl.when(has_up)
        def _():
            action(1)

    both(lambda side: halo(side).start())
    for t in range(1, strata):
        for k in range(4):
            edge(t, k).start()

    def counts(t):
        if t == 0:
            a, b_, c, d = e_src.at[0], e_tgt.at[0], e_w.at[0], e_neg.at[0]
        else:
            for k in range(4):
                edge(t, k).wait_recv()
            a, b_, c, d = r_src.at[t - 1], r_tgt.at[t - 1], r_w.at[t - 1], r_neg.at[t - 1]

        @pl.loop(0, blocks, unroll=2)
        def _(b):
            one = pl.ds(b, 1)
            count_tile(b, a[one, :], b_[one, :], c[one, :], jnp.concatenate([d[n, one, :] for n in range(d.shape[0])], axis=0), wneg.at[t % 2], wpos.at[t % 2], rowblk)

    for slot in range(2):
        for h in range(chunks):
            wpos[slot, h] = jnp.zeros((rows, LANE), F32)
    counts(0)

    cext[STRIP : STRIP + rows] = c_in[...]
    for side in range(2):
        there = has_down if side == 0 else has_up
        span = slice(0, STRIP) if side == 0 else slice(STRIP + rows, rows + 2 * STRIP)

        @pl.when(there)
        def _():
            halo(1 - side).wait_recv()
            cext[span] = chalo[side]

        @pl.when(jnp.logical_not(there))
        def _():
            cext[span] = jnp.zeros((STRIP, width), F32)

    def chunk(slot, h, r0, nrows):
        part = slice(r0, r0 + nrows)
        c = cext[pl.ds(pl.multiple_of(h * LANE, LANE), LANE), :]
        chi, clo = split(c)
        cc = jnp.concatenate([chi, chi], axis=1)
        ccat = jnp.concatenate([chi, clo], axis=1)
        score = dot(vcat[part], cc, NT) + dot(vcat[part, :width], clo, NT)
        sig = 0.5 * jnp.tanh(0.5 * score) + 0.5
        pos = wpos[slot, h, part, :]
        gg = wneg[slot, h, part, :] * sig + pos * (sig - 1.0)
        g1, g2 = split(gg)
        wide = dot(g1, ccat)
        gv[part] += wide[:, :width] + wide[:, width:] + dot(g2, chi)
        tall = dot(vtcat[:, part], g1)
        gt = tall[:width] + tall[width:] + dot(vtcat[:width, part], g2)
        return gt.T

    for t in range(strata):
        slot = t % 2
        if t == 0:
            v_now = v_in
        else:
            for part in range(2):
                hop(t - 1, part).wait_recv()
            v_now = vrecv.at[t - 1]
        v = v_now[...]
        vhi, vlo = split(v)
        vcat[...] = jnp.concatenate([vhi, vlo], axis=1)
        vcat_t = split(v.T)
        vtcat[...] = jnp.concatenate(vcat_t, axis=0)
        gv[...] = jnp.zeros((rows, width), F32)
        far = gray(t) ^ gray((t + 1) % strata) > 1
        parts = 2 if far else 1
        nrows = rows // parts
        for part in range(parts):
            r0 = part * nrows

            @pl.loop(0, 4, unroll=2)
            def _(j):
                side = j // 2
                span = pl.ds(pl.multiple_of((j % 2) * LANE, LANE), LANE)
                gt = chunk(slot, j + 2 * side, r0, nrows)
                if part == 0:
                    gs[t, side, span, :] = gt
                else:
                    gs[t, side, span, :] += gt

            if part == parts - 1:
                both(lambda side: rim(t, side).start())

            @pl.loop(0, 2, unroll=2)
            def _(j):
                span = pl.ds(pl.multiple_of(j * LANE, LANE), LANE)
                gt = chunk(slot, j + 2, r0, nrows)
                if part == 0:
                    gm[span, :] = gt
                else:
                    gm[span, :] += gt

            mine = slice(r0, r0 + nrows)
            vnew[t, mine] = v_now[mine] - LR * gv[mine]
            for half in range(2) if parts == 1 else (part,):
                hop(t, half).start()
        if t < strata - 1:
            cext[zone : zone + rows - zone] -= LR * gm[...]
            counts(t + 1)
            for side in range(2):
                there = has_down if side == 0 else has_up
                base = 0 if side == 0 else rows
                own = slice(base + STRIP, base + zone) if side == 0 else slice(base, base + STRIP)
                off = slice(STRIP, zone) if side == 0 else slice(0, STRIP)

                @pl.when(there)
                def _():
                    rim(t, 1 - side).wait_recv()
                    cext[base : base + zone] -= LR * (gs[t, side] + gr[t, side])

                @pl.when(jnp.logical_not(there))
                def _():
                    cext[own] -= LR * gs[t, side, off]
        else:
            cout[STRIP : rows - STRIP] = cext[zone:rows] - LR * gm[...]
            for side in range(2):
                there = has_down if side == 0 else has_up
                base = 0 if side == 0 else rows
                own = slice(base + STRIP, base + zone) if side == 0 else slice(base, base + STRIP)
                off = slice(STRIP, zone) if side == 0 else slice(0, STRIP)
                to = slice(0, STRIP) if side == 0 else slice(rows - STRIP, rows)

                @pl.when(there)
                def _():
                    rim(t, 1 - side).wait_recv()
                    cout[to] = cext[own] - LR * (gs[t, side, off] + gr[t, side, off])

                @pl.when(jnp.logical_not(there))
                def _():
                    cout[to] = cext[own] - LR * gs[t, side, off]

            for part in range(2):
                hop(t, part).wait_recv()
            vout[...] = vrecv[t]

    both(lambda side: halo(side).wait_send())
    for t in range(strata):
        both(lambda side: rim(t, side).wait_send())
        for part in range(2):
            hop(t, part).wait_send()
        if t:
            for k in range(4):
                edge(t, k).wait_send()


def hand_on(v, c, vout, cout):
    vout[...] = v[...]
    cout[...] = c[...]


def local(vertex, context, edge_source, edge_target, edge_weight, negative_rows):
    strata, _, blocks, slots = edge_source.shape
    negs = negative_rows.shape[3]
    rows, width = vertex.shape
    ext = rows + 2 * STRIP
    chunks = ext // LANE
    flat = (strata, blocks, slots)
    vm = pl.BlockSpec(memory_space=pltpu.VMEM)
    sem = pltpu.SemaphoreType.DMA
    i32 = jnp.int32
    final = pl.pallas_call(
        kernel,
        out_shape=(jax.ShapeDtypeStruct((rows, width), F32),) * 2,
        in_specs=[vm] * 6,
        out_specs=(vm, vm),
        scratch_shapes=[
            pltpu.VMEM((2, chunks, rows, LANE), F32),
            pltpu.VMEM((2, chunks, rows, LANE), F32),
            pltpu.VMEM((strata - 1, blocks, slots), i32),
            pltpu.VMEM((strata - 1, blocks, slots), i32),
            pltpu.VMEM((strata - 1, blocks, slots), i32),
            pltpu.VMEM((strata - 1, negs, blocks, slots), i32),
            pltpu.VMEM((strata, rows, width), F32),
            pltpu.VMEM((strata, rows, width), F32),
            pltpu.VMEM((strata, 2, 2 * STRIP, width), F32),
            pltpu.VMEM((strata, 2, 2 * STRIP, width), F32),
            pltpu.VMEM((rows - 2 * STRIP, width), F32),
            pltpu.VMEM((rows, width), F32),
            pltpu.VMEM((ext, width), F32),
            pltpu.VMEM((2, STRIP, width), F32),
            pltpu.VMEM((rows, 2 * width), BF),
            pltpu.VMEM((2 * width, rows), BF),
            sem((4 * (strata - 1),)),
            sem((4 * (strata - 1),)),
            sem((2,)),
            sem((2,)),
            sem((strata, 2)),
            sem((strata, 2)),
            sem((strata, 2)),
            sem((strata, 2)),
        ],
        compiler_params=pltpu.CompilerParams(
            collective_id=0, has_side_effects=True, vmem_limit_bytes=60 * 1024 * 1024
        ),
    )(
        vertex,
        context,
        edge_source.reshape(flat),
        edge_target.reshape(flat),
        edge_weight.reshape(flat),
        negative_rows.reshape(strata, blocks, negs, slots).transpose(0, 2, 1, 3),
    )
    return pl.pallas_call(
        hand_on,
        out_shape=(jax.ShapeDtypeStruct((rows, width), F32),) * 2,
        in_specs=[vm] * 2,
        out_specs=(vm, vm),
    )(*final)


def solution(mesh):
    lead = P(("grp", "mem"), None)
    edges = P(None, "grp", "mem", None)
    return jax.shard_map(
        local,
        mesh=mesh,
        in_specs=(lead, lead, edges, edges, edges, P(None, "grp", "mem", None, None)),
        out_specs=(lead, lead),
        check_vma=False,
    )
```

profile of v0, /device:TPU:16, one launch (start us, length us, event | category | flops | bytes accessed | tf_op | source)
XLA Modules:
  0.0 92.5 jit_solution(1195767811963071277)
XLA Ops:
  0.6 89.7 %shard_map.77 = (f32[1024,128]{1,0:T(8,128)}, f32[1024,128]{1,0:T(8,128)}) custom-call(f32[1024,128]{1,0:T(8,128)} %v_in.1, f32[1024,128]{1,0:T(8,128)} %c_in.1, s32[4,8,512]{2,1,0:T(8,128)} %bitcast.7, s32[4,8,512]{2,1,0:T(8,128)} %bitcast.8, s32[4,8,512]{2,1,0:T(8,128)} %bitcast.9, s32[4,5,8,512]{3,2,1,0:T(8,128)} %bitcast.6), custom_call_target="tpu_custom_call" | custom-call | tf_op jit(solution)/shard_map/pallas_call | solution.py:312
  90.3 2.2 %shard_map.78 = (f32[1024,128]{1,0:T(8,128)}, f32[1024,128]{1,0:T(8,128)}) custom-call(f32[1024,128]{1,0:T(8,128)} %get-tuple-element.4.v, f32[1024,128]{1,0:T(8,128)} %get-tuple-element.5.c), custom_call_target="tpu_custom_call" | custom-call | tf_op jit(solution)/shard_map/pallas_call | solution.py:354
where the time goes:
time: 92.7 us; the launch traced here: 92.5 us
  Pallas kernels  91.9 us (99%)
    pallas_call x1, Pallas kernels, local(): pl.pallas_call(kernel, out_shape=(jax.ShapeDtypeStruct((rows, width), F32...  89.7 us
    pallas_call x1, Pallas kernels, local(): pl.pallas_call(hand_on, out_shape=(jax.ShapeDtypeStruct((rows, width), F3...  2.2 us

commit v1 on v0

--- a/solution.py
+++ b/solution.py
@@ -11,6 +11,7 @@
 STRIP = 256
 LANE = 256
 BF = jnp.bfloat16
+F8 = jnp.float8_e4m3fn
 F32 = jnp.float32
 NT = (((1,), (1,)), ((), ()))
 NN = (((1,), (0,)), ((), ()))
@@ -39,12 +40,12 @@
     s1 = jnp.where(iota_r == row_bf(src), row_bf(w), zero)
 
     def hot(x):
-        return jnp.where(iota_c == row_bf(x & (LANE - 1)), one, zero)
+        return jnp.where(iota_c == row_bf(x & (LANE - 1)), one, zero).astype(F8)
 
     def tall(x, first, count):
         hi = (x >> 8) - first
         return jnp.concatenate(
-            [s1 * row_bf(jnp.where(hi == h, 1.0, 0.0)) for h in range(count)], axis=0
+            [(s1 * row_bf(jnp.where(hi == h, 1.0, 0.0))).astype(F8) for h in range(count)], axis=0
         )
 
     at = jnp.concatenate([tall(neg[n : n + 1], 0, chunks) for n in range(neg.shape[0])], axis=1)

time: 92.7 us -> 88.2 us (0.951)
  Pallas kernels: 91.9 us -> 87.2 us
    pallas_call x1, Pallas kernels: 89.7 us -> 85 us  [local(): pl.pallas_call(kernel, out_shape=(jax.ShapeDtypeStruct((rows, width), F32...]
where the time goes in v1:
time: 88.2 us; the launch traced here: 87.8 us
  Pallas kernels  87.2 us (99%)
    pallas_call x1, Pallas kernels, local(): pl.pallas_call(kernel, out_shape=(jax.ShapeDtypeStruct((rows, width), F32...  85 us
    pallas_call x1, Pallas kernels, local(): pl.pallas_call(hand_on, out_shape=(jax.ShapeDtypeStruct((rows, width), F3...  2.2 us

profile of v1, /device:TPU:16, one launch (start us, length us, event | category | flops | bytes accessed | tf_op | source)
XLA Modules:
  0.0 87.8 jit_solution(11932546905762852109)
XLA Ops:
  0.6 85.0 %shard_map.77 = (f32[1024,128]{1,0:T(8,128)}, f32[1024,128]{1,0:T(8,128)}) custom-call(f32[1024,128]{1,0:T(8,128)} %v_in.1, f32[1024,128]{1,0:T(8,128)} %c_in.1, s32[4,8,512]{2,1,0:T(8,128)} %bitcast.7, s32[4,8,512]{2,1,0:T(8,128)} %bitcast.8, s32[4,8,512]{2,1,0:T(8,128)} %bitcast.9, s32[4,5,8,512]{3,2,1,0:T(8,128)} %bitcast.6), custom_call_target="tpu_custom_call" | custom-call | tf_op jit(solution)/shard_map/pallas_call | solution.py:313
  85.6 2.2 %shard_map.78 = (f32[1024,128]{1,0:T(8,128)}, f32[1024,128]{1,0:T(8,128)}) custom-call(f32[1024,128]{1,0:T(8,128)} %get-tuple-element.4.v, f32[1024,128]{1,0:T(8,128)} %get-tuple-element.5.c), custom_call_target="tpu_custom_call" | custom-call | tf_op jit(solution)/shard_map/pallas_call | solution.py:355

commit v2 on v1

v2 whole, which is shorter than its diff:
```python
import functools

import jax
import jax.numpy as jnp
from jax import lax
from jax.experimental import pallas as pl
from jax.experimental.pallas import tpu as pltpu
from jax.sharding import PartitionSpec as P

LR = 0.05
STRIP = 256
LANE = 256
BF = jnp.bfloat16
F8 = jnp.float8_e4m3fn
F32 = jnp.float32
NT = (((1,), (1,)), ((), ()))
NN = (((1,), (0,)), ((), ()))
TN = (((0,), (0,)), ((), ()))
UP = 256.0
TOP = 448.0


def dot(a, b, dims=NN):
    return lax.dot_general(a, b, dims, preferred_element_type=F32)


def split(x):
    hi = x.astype(BF)
    return hi, (x - hi.astype(F32)).astype(BF)


def small(x, scale):
    return jnp.clip(x.astype(F32) * scale, -TOP, TOP).astype(F8)


def row_bf(x):
    return x.astype(F32).astype(BF)


def count_tile(b, src, tgt, w, neg, wsum, wdif, rowblk):
    slots = src.shape[1]
    chunks = wsum.shape[0]
    one = jnp.ones((), BF)
    zero = jnp.zeros((), BF)
    iota_r = row_bf(lax.broadcasted_iota(jnp.int32, (rowblk, slots), 0))
    iota_c = row_bf(lax.broadcasted_iota(jnp.int32, (LANE, slots), 0))
    s1 = jnp.where(iota_r == row_bf(src), row_bf(w) * jnp.asarray(0.5, BF), zero)

    def hot(x):
        return jnp.where(iota_c == row_bf(x & (LANE - 1)), one, zero).astype(F8)

    def tall(x, first, count):
        hi = (x >> 8) - first
        return jnp.concatenate(
            [(s1 * row_bf(jnp.where(hi == h, 1.0, 0.0))).astype(F8) for h in range(count)], axis=0
        )

    at = jnp.concatenate([tall(neg[n : n + 1], 0, chunks) for n in range(neg.shape[0])], axis=1)
    bt = jnp.concatenate([hot(neg[n : n + 1]) for n in range(neg.shape[0])], axis=1)
    cn = dot(at, bt, NT)
    first = b // 2
    cp = dot(tall(tgt, first, 3), hot(tgt), NT)
    rows = pl.ds(pl.multiple_of(b * rowblk, rowblk), rowblk)
    for h in range(chunks):
        wsum[h, rows, :] = cn[h * rowblk : (h + 1) * rowblk]
        wdif[h, rows, :] = cn[h * rowblk : (h + 1) * rowblk]
    for h in range(3):
        wsum[first + h, rows, :] += cp[h * rowblk : (h + 1) * rowblk]
        wdif[first + h, rows, :] -= cp[h * rowblk : (h + 1) * rowblk]


def flip(g, value):
    bit = 1
    while bit <= value:
        if value & bit:
            g = g + bit - 2 * bit * ((g // bit) % 2)
        bit *= 2
    return g


def gray(t):
    return t ^ (t >> 1)


def remote(src, dst, send, recv, **where):
    return pltpu.make_async_remote_copy(
        src_ref=src, dst_ref=dst, send_sem=send, recv_sem=recv,
        device_id=where, device_id_type=pl.DeviceIdType.MESH,
    )


def kernel(
    v_in, c_in, e_src, e_tgt, e_w, e_neg, vout, cout,
    wsum, wdif, r_src, r_tgt, r_w, r_neg, vnew, vrecv, gs, gr, gm, gv, cext, cnext, clast, cfin, chalo, vcat, v8,
    edge_send, edge_recv, halo_send, halo_recv, rim_send, rim_recv, v_send, v_recv, c_send, c_recv,
):
    strata, blocks, slots = e_src.shape
    rows, width = v_in.shape
    rowblk = rows // blocks
    chunks = wsum.shape[1]
    zone = 2 * STRIP
    g = lax.axis_index("grp")
    m = lax.axis_index("mem")
    members = lax.axis_size("mem")
    has_down = m > 0
    has_up = m < members - 1
    near, far = flip(g, 1), flip(g, 2)

    barrier = pltpu.get_barrier_semaphore()
    for partner in (near, far):
        pl.semaphore_signal(barrier, inc=1, device_id={"grp": partner}, device_id_type=pl.DeviceIdType.MESH)

    @pl.when(has_down)
    def _():
        pl.semaphore_signal(barrier, inc=1, device_id={"mem": m - 1}, device_id_type=pl.DeviceIdType.MESH)

    @pl.when(has_up)
    def _():
        pl.semaphore_signal(barrier, inc=1, device_id={"mem": m + 1}, device_id_type=pl.DeviceIdType.MESH)

    pl.semaphore_wait(barrier, 2 + jnp.where(has_down, 1, 0) + jnp.where(has_up, 1, 0))

    def halo(side):
        if side == 0:
            return remote(c_in.at[0:STRIP], chalo.at[1], halo_send.at[0], halo_recv.at[1], mem=m - 1)
        return remote(c_in.at[rows - STRIP : rows], chalo.at[0], halo_send.at[1], halo_recv.at[0], mem=m + 1)

    def rim(t, side):
        last = t == strata - 1
        if side == 0:
            span = slice(0, STRIP if last else zone)
            return remote(gs.at[t, 0, span], gr.at[t, 1, span], rim_send.at[t, 0], rim_recv.at[t, 1], mem=m - 1)
        span = slice(STRIP if last else 0, zone)
        return remote(gs.at[t, 1, span], gr.at[t, 0, span], rim_send.at[t, 1], rim_recv.at[t, 0], mem=m + 1)

    def hop(t):
        i = t // 2
        return remote(vnew.at[i], vrecv.at[i], v_send.at[i], v_recv.at[i], grp=near)

    def area(side):
        return slice(zone, rows) if side == 2 else slice(side * rows, side * rows + zone)

    def own(side):
        return (slice(0, STRIP), slice(rows - STRIP, rows), slice(STRIP, rows - STRIP))[side]

    def cross(side):
        span = area(side)
        return remote(cext.at[span], cnext.at[span], c_send.at[0, side], c_recv.at[0, side], grp=far)

    def home(side):
        span = own(side)
        return remote(clast.at[span], cfin.at[span], c_send.at[1, side], c_recv.at[1, side], grp=far)

    def edge(t, k):
        a = (e_src, e_tgt, e_w, e_neg)[k]
        z = (r_src, r_tgt, r_w, r_neg)[k]
        i = (t - 1) * 4 + k
        return remote(a.at[t], z.at[t - 1], edge_send.at[i], edge_recv.at[i], grp=near)

    def guard(side, action):
        @pl.when(has_down if side == 0 else has_up)
        def _():
            action()

    def counts(t, between=None):
        if t in (0, strata - 1):
            a, b_, c, d = e_src.at[t], e_tgt.at[t], e_w.at[t], e_neg.at[t]
        else:
            for k in range(4):
                edge(t, k).wait_recv()
            a, b_, c, d = r_src.at[t - 1], r_tgt.at[t - 1], r_w.at[t - 1], r_neg.at[t - 1]

        def run(lo, hi):
            @pl.loop(lo, hi, unroll=2)
            def _(b):
                one = pl.ds(b, 1)
                count_tile(b, a[one, :], b_[one, :], c[one, :], jnp.concatenate([d[n, one, :] for n in range(d.shape[0])], axis=0), wsum.at[t % 2], wdif.at[t % 2], rowblk)

        if between is None:
            run(0, blocks)
        else:
            run(0, blocks // 2)
            between()
            run(blocks // 2, blocks)

    def enter(side):
        there = has_down if side == 0 else has_up
        span = slice(0, STRIP) if side == 0 else slice(STRIP + rows, rows + 2 * STRIP)

        @pl.when(there)
        def _():
            halo(1 - side).wait_recv()
            cext[span] = chalo[side]

        @pl.when(jnp.logical_not(there))
        def _():
            cext[span] = jnp.zeros((STRIP, width), F32)

    def settle(t, side, ctx):
        there = has_down if side == 0 else has_up
        base = side * rows
        mine = slice(base + STRIP, base + zone) if side == 0 else slice(base, base + STRIP)
        off = slice(STRIP, zone) if side == 0 else slice(0, STRIP)

        @pl.when(there)
        def _():
            rim(t, 1 - side).wait_recv()
            ctx[base : base + zone] -= LR * (gs[t, side] + gr[t, side])

        @pl.when(jnp.logical_not(there))
        def _():
            ctx[mine] -= LR * gs[t, side, off]

    def finish(side):
        t = strata - 1
        there = has_down if side == 0 else has_up
        base = side * rows
        mine = slice(base + STRIP, base + zone) if side == 0 else slice(base, base + STRIP)
        off = slice(STRIP, zone) if side == 0 else slice(0, STRIP)
        to = own(side)

        @pl.when(there)
        def _():
            rim(t, 1 - side).wait_recv()
            clast[to] = cnext[mine] - LR * (gs[t, side, off] + gr[t, side, off])

        @pl.when(jnp.logical_not(there))
        def _():
            clast[to] = cnext[mine] - LR * gs[t, side, off]

        home(side).start()

    def chunk(slot, ctx, h):
        c = ctx[pl.ds(pl.multiple_of(h * LANE, LANE), LANE), :]
        chi, clo = split(c)
        ccat = jnp.concatenate([chi, clo], axis=1)
        chalf = (chi.astype(F32) * 0.5).astype(BF)
        c8 = jnp.concatenate([small(chi, 0.5), small(clo, 0.5 * UP)], axis=1)
        half = dot(vcat[:, :width], chalf, NT) + dot(v8[...], c8, NT) * (1.0 / UP)
        gg = wsum[slot, h] * jnp.tanh(half) + wdif[slot, h]
        g1, g2 = split(gg)
        wide = dot(g1, ccat)
        gv[...] += wide[:, :width] + wide[:, width:] + dot(g2, chi)
        tall = dot(g1, vcat[...], TN)
        return tall[:, :width] + tall[:, width:] + dot(g2, vcat[:, :width], TN)

    def sweep(slot, ctx, first, count, into):
        @pl.loop(0, count, unroll=2)
        def _(j):
            into[pl.ds(pl.multiple_of(j * LANE, LANE), LANE), :] = chunk(slot, ctx, first + j)

    def take(v):
        vhi, vlo = split(v)
        vcat[...] = jnp.concatenate([vhi, vlo], axis=1)
        v8[...] = jnp.concatenate([small(vlo, UP), small(vhi, 1.0)], axis=1)
        gv[...] = jnp.zeros((rows, width), F32)

    def middle(t, ctx):
        sweep(t % 2, ctx, 2, chunks - 4, gm)

    def rims(t, side, ctx):
        sweep(t % 2, ctx, side * (chunks - 2), 2, gs.at[t, side])
        guard(side, lambda: rim(t, side).start())

    guard(1, lambda: halo(1).start())
    for k in range(4):
        edge(1, k).start()
    counts(0, lambda: guard(0, lambda: halo(0).start()))
    for k in range(4):
        edge(2, k).start()

    cext[STRIP : STRIP + rows] = c_in[...]
    take(v_in[...])
    enter(0)
    rims(0, 0, cext)
    middle(0, cext)
    enter(1)
    rims(0, 1, cext)
    vnew[0] = v_in[...] - LR * gv[...]
    hop(0).start()
    cext[zone:rows] -= LR * gm[...]
    counts(1)

    hop(0).wait_recv()
    take(vrecv[0])
    middle(1, cext)
    cext[zone:rows] -= LR * gm[...]
    cross(2).start()
    for side in (1, 0):
        settle(0, side, cext)
        rims(1, side, cext)
    stay = vrecv[0] - LR * gv[...]
    vrecv[0] = stay
    take(stay)
    counts(2)

    settle(1, 0, cext)
    cross(0).start()
    cross(2).wait_recv()
    middle(2, cnext)
    cnext[zone:rows] -= LR * gm[...]
    settle(1, 1, cext)
    cross(1).start()
    for side in (0, 1):
        cross(side).wait_recv()
        rims(2, side, cnext)
    vnew[1] = vrecv[0] - LR * gv[...]
    hop(2).start()
    counts(3)

    hop(2).wait_recv()
    take(vrecv[1])
    middle(3, cnext)
    clast[own(2)] = cnext[zone:rows] - LR * gm[...]
    home(2).start()
    for side in (1, 0):
        settle(2, side, cnext)
        rims(3, side, cnext)
    vout[...] = vrecv[1] - LR * gv[...]
    for side in (0, 1):
        finish(side)
    for side in (2, 0, 1):
        home(side).wait_recv()
        cout[own(side)] = cfin[own(side)]

    for side in range(2):
        guard(side, lambda: halo(side).wait_send())
    for t in range(strata):
        for side in range(2):
            guard(side, lambda: rim(t, side).wait_send())
    for t in (0, 2):
        hop(t).wait_send()
    for t in (1, 2):
        for k in range(4):
            edge(t, k).wait_send()
    for side in range(3):
        cross(side).wait_send()
        home(side).wait_send()


def hand_on(v, c, vout, cout):
    vout[...] = v[...]
    cout[...] = c[...]


def local(vertex, context, edge_source, edge_target, edge_weight, negative_rows):
    strata, _, blocks, slots = edge_source.shape
    negs = negative_rows.shape[3]
    rows, width = vertex.shape
    ext = rows + 2 * STRIP
    chunks = ext // LANE
    flat = (strata, blocks, slots)
    vm = pl.BlockSpec(memory_space=pltpu.VMEM)
    sem = pltpu.SemaphoreType.DMA
    i32 = jnp.int32
    final = pl.pallas_call(
        kernel,
        out_shape=(jax.ShapeDtypeStruct((rows, width), F32),) * 2,
        in_specs=[vm] * 6,
        out_specs=(vm, vm),
        scratch_shapes=[
            pltpu.VMEM((2, chunks, rows, LANE), F32),
            pltpu.VMEM((2, chunks, rows, LANE), F32),
            pltpu.VMEM((2, blocks, slots), i32),
            pltpu.VMEM((2, blocks, slots), i32),
            pltpu.VMEM((2, blocks, slots), i32),
            pltpu.VMEM((2, negs, blocks, slots), i32),
            pltpu.VMEM((2, rows, width), F32),
            pltpu.VMEM((2, rows, width), F32),
            pltpu.VMEM((strata, 2, 2 * STRIP, width), F32),
            pltpu.VMEM((strata, 2, 2 * STRIP, width), F32),
            pltpu.VMEM((rows - 2 * STRIP, width), F32),
            pltpu.VMEM((rows, width), F32),
            pltpu.VMEM((ext, width), F32),
            pltpu.VMEM((ext, width), F32),
            pltpu.VMEM((rows, width), F32),
            pltpu.VMEM((rows, width), F32),
            pltpu.VMEM((2, STRIP, width), F32),
            pltpu.VMEM((rows, 2 * width), BF),
            pltpu.VMEM((rows, 2 * width), F8),
            sem((8,)),
            sem((8,)),
            sem((2,)),
            sem((2,)),
            sem((strata, 2)),
            sem((strata, 2)),
            sem((2,)),
            sem((2,)),
            sem((2, 3)),
            sem((2, 3)),
        ],
        compiler_params=pltpu.CompilerParams(
            collective_id=0, has_side_effects=True, vmem_limit_bytes=60 * 1024 * 1024
        ),
    )(
        vertex,
        context,
        edge_source.reshape(flat),
        edge_target.reshape(flat),
        edge_weight.reshape(flat),
        negative_rows.reshape(strata, blocks, negs, slots).transpose(0, 2, 1, 3),
    )
    return pl.pallas_call(
        hand_on,
        out_shape=(jax.ShapeDtypeStruct((rows, width), F32),) * 2,
        in_specs=[vm] * 2,
        out_specs=(vm, vm),
    )(*final)


def solution(mesh):
    lead = P(("grp", "mem"), None)
    edges = P(None, "grp", "mem", None)
    return jax.shard_map(
        local,
        mesh=mesh,
        in_specs=(lead, lead, edges, edges, edges, P(None, "grp", "mem", None, None)),
        out_specs=(lead, lead),
        check_vma=False,
    )
```

time: 88.2 us -> 75.2 us (0.85)
  Pallas kernels: 87.2 us -> 74 us
    pallas_call x1, Pallas kernels: 85 us -> 71.8 us  [local(): pl.pallas_call(kernel, out_shape=(jax.ShapeDtypeStruct((rows, width), F32...]
where the time goes in v2:
time: 75.2 us; the launch traced here: 74.7 us
  Pallas kernels  74 us (98%)
    pallas_call x1, Pallas kernels, local(): pl.pallas_call(kernel, out_shape=(jax.ShapeDtypeStruct((rows, width), F32...  71.8 us
    pallas_call x1, Pallas kernels, local(): pl.pallas_call(hand_on, out_shape=(jax.ShapeDtypeStruct((rows, width), F3...  2.2 us

profile of v2, /device:TPU:16, one launch (start us, length us, event | category | flops | bytes accessed | tf_op | source)
XLA Modules:
  0.0 74.7 jit_solution(4400101797049142451)
XLA Ops:
  0.6 71.8 %shard_map.77 = (f32[1024,128]{1,0:T(8,128)}, f32[1024,128]{1,0:T(8,128)}) custom-call(f32[1024,128]{1,0:T(8,128)} %v_in.1, f32[1024,128]{1,0:T(8,128)} %c_in.1, s32[4,8,512]{2,1,0:T(8,128)} %bitcast.7, s32[4,8,512]{2,1,0:T(8,128)} %bitcast.8, s32[4,8,512]{2,1,0:T(8,128)} %bitcast.9, s32[4,5,8,512]{3,2,1,0:T(8,128)} %bitcast.6), custom_call_target="tpu_custom_call" | custom-call | tf_op jit(solution)/shard_map/pallas_call | solution.py:356
  72.5 2.2 %shard_map.78 = (f32[1024,128]{1,0:T(8,128)}, f32[1024,128]{1,0:T(8,128)}) custom-call(f32[1024,128]{1,0:T(8,128)} %get-tuple-element.4.v, f32[1024,128]{1,0:T(8,128)} %get-tuple-element.5.c), custom_call_target="tpu_custom_call" | custom-call | tf_op jit(solution)/shard_map/pallas_call | solution.py:403

commit v3 on v2

--- a/solution.py
+++ b/solution.py
@@ -162,7 +162,7 @@
         def _():
             action()
 
-    def counts(t, between=None):
+    def counts(t, between=None, cut=4):
         if t in (0, strata - 1):
             a, b_, c, d = e_src.at[t], e_tgt.at[t], e_w.at[t], e_neg.at[t]
         else:
@@ -179,9 +179,9 @@
         if between is None:
             run(0, blocks)
         else:
-            run(0, blocks // 2)
+            run(0, blocks * cut // 8)
             between()
-            run(blocks // 2, blocks)
+            run(blocks * cut // 8, blocks)
 
     def enter(side):
         there = has_down if side == 0 else has_up
@@ -283,30 +283,36 @@
 
     hop(0).wait_recv()
     take(vrecv[0])
+    settle(0, 1, cext)
+    rims(1, 1, cext)
     middle(1, cext)
     cext[zone:rows] -= LR * gm[...]
     cross(2).start()
-    for side in (1, 0):
-        settle(0, side, cext)
-        rims(1, side, cext)
+    settle(0, 0, cext)
+    rims(1, 0, cext)
     stay = vrecv[0] - LR * gv[...]
     vrecv[0] = stay
     take(stay)
-    counts(2)
-
-    settle(1, 0, cext)
-    cross(0).start()
+    def pass_on():
+        settle(1, 0, cext)
+        cross(0).start()
+
+    counts(2, pass_on)
     cross(2).wait_recv()
+    settle(1, 1, cext)
+    cross(1).start()
     middle(2, cnext)
     cnext[zone:rows] -= LR * gm[...]
-    settle(1, 1, cext)
-    cross(1).start()
-    for side in (0, 1):
-        cross(side).wait_recv()
-        rims(2, side, cnext)
-    vnew[1] = vrecv[0] - LR * gv[...]
-    hop(2).start()
-    counts(3)
+    cross(0).wait_recv()
+    rims(2, 0, cnext)
+
+    def last_zone():
+        cross(1).wait_recv()
+        rims(2, 1, cnext)
+        vnew[1] = vrecv[0] - LR * gv[...]
+        hop(2).start()
+
+    counts(3, last_zone, 2)
 
     hop(2).wait_recv()
     take(vrecv[1])

time: 75.2 us -> 71.8 us (0.955)
  Pallas kernels: 74 us -> 70 us
    pallas_call x1, Pallas kernels: 71.8 us -> 67.8 us  [local(): pl.pallas_call(kernel, out_shape=(jax.ShapeDtypeStruct((rows, width), F32...]
where the time goes in v3:
time: 71.8 us; the launch traced here: 70.7 us
  Pallas kernels  70 us (97%)
    pallas_call x1, Pallas kernels, local(): pl.pallas_call(kernel, out_shape=(jax.ShapeDtypeStruct((rows, width), F32...  67.8 us
    pallas_call x1, Pallas kernels, local(): pl.pallas_call(hand_on, out_shape=(jax.ShapeDtypeStruct((rows, width), F3...  2.2 us

profile of v3, /device:TPU:16, one launch (start us, length us, event | category | flops | bytes accessed | tf_op | source)
XLA Modules:
  0.0 70.7 jit_solution(8791268603180678323)
XLA Ops:
  0.6 67.8 %shard_map.77 = (f32[1024,128]{1,0:T(8,128)}, f32[1024,128]{1,0:T(8,128)}) custom-call(f32[1024,128]{1,0:T(8,128)} %v_in.1, f32[1024,128]{1,0:T(8,128)} %c_in.1, s32[4,8,512]{2,1,0:T(8,128)} %bitcast.7, s32[4,8,512]{2,1,0:T(8,128)} %bitcast.8, s32[4,8,512]{2,1,0:T(8,128)} %bitcast.9, s32[4,5,8,512]{3,2,1,0:T(8,128)} %bitcast.6), custom_call_target="tpu_custom_call" | custom-call | tf_op jit(solution)/shard_map/pallas_call | solution.py:362
  68.5 2.2 %shard_map.78 = (f32[1024,128]{1,0:T(8,128)}, f32[1024,128]{1,0:T(8,128)}) custom-call(f32[1024,128]{1,0:T(8,128)} %get-tuple-element.4.v, f32[1024,128]{1,0:T(8,128)} %get-tuple-element.5.c), custom_call_target="tpu_custom_call" | custom-call | tf_op jit(solution)/shard_map/pallas_call | solution.py:409

commit v4 on v3

--- a/solution.py
+++ b/solution.py
@@ -297,7 +297,7 @@
         settle(1, 0, cext)
         cross(0).start()
 
-    counts(2, pass_on)
+    counts(2, pass_on, 2)
     cross(2).wait_recv()
     settle(1, 1, cext)
     cross(1).start()

time: 71.8 us -> 72.1 us (level)
  Pallas kernels: 70 us -> 71 us
    pallas_call x1, Pallas kernels: 67.8 us -> 68.8 us  [local(): pl.pallas_call(kernel, out_shape=(jax.ShapeDtypeStruct((rows, width), F32...]
where the time goes in v4:
time: 72.1 us; the launch traced here: 71.7 us
  Pallas kernels  71 us (98%)
    pallas_call x1, Pallas kernels, local(): pl.pallas_call(kernel, out_shape=(jax.ShapeDtypeStruct((rows, width), F32...  68.8 us
    pallas_call x1, Pallas kernels, local(): pl.pallas_call(hand_on, out_shape=(jax.ShapeDtypeStruct((rows, width), F3...  2.2 us

profile of v4, /device:TPU:16, one launch (start us, length us, event | category | flops | bytes accessed | tf_op | source)
XLA Modules:
  0.0 71.7 jit_solution(16366621975706994452)
XLA Ops:
  0.6 68.8 %shard_map.77 = (f32[1024,128]{1,0:T(8,128)}, f32[1024,128]{1,0:T(8,128)}) custom-call(f32[1024,128]{1,0:T(8,128)} %v_in.1, f32[1024,128]{1,0:T(8,128)} %c_in.1, s32[4,8,512]{2,1,0:T(8,128)} %bitcast.7, s32[4,8,512]{2,1,0:T(8,128)} %bitcast.8, s32[4,8,512]{2,1,0:T(8,128)} %bitcast.9, s32[4,5,8,512]{3,2,1,0:T(8,128)} %bitcast.6), custom_call_target="tpu_custom_call" | custom-call | tf_op jit(solution)/shard_map/pallas_call | solution.py:362
  69.5 2.2 %shard_map.78 = (f32[1024,128]{1,0:T(8,128)}, f32[1024,128]{1,0:T(8,128)}) custom-call(f32[1024,128]{1,0:T(8,128)} %get-tuple-element.4.v, f32[1024,128]{1,0:T(8,128)} %get-tuple-element.5.c), custom_call_target="tpu_custom_call" | custom-call | tf_op jit(solution)/shard_map/pallas_call | solution.py:409
